TPU v7x, 256 devices: a whole 4x4x8 slice. The times are simulated.
256 devices in a mesh: dp: 32 (over y, z_hi, x), mp: 8 (over z_lo, core).
Axes of the slice: x: 4, y: 4, z: 8 (z_hi: 2, z_lo: 4; z = z_hi * 4 + z_lo), core: 2. Of those that a mesh axis runs over, the one named last changes fastest.
Arguments:
- acts: bfloat16 [1, 131072, 8192], P(None, 'dp', 'mp'), may hold values from -6 to 6
- rank_space_gradient: bfloat16 [1, 131072, 16], P(None, 'dp'), may hold values from -0.15625 to 0.15625
- running_factor_blocks: float32 [8, 1024, 1024], P('mp', 'dp')
- inverse_root_blocks: float32 [8, 1024, 1024], P('mp', 'dp')
- owner_block_order: int32 [8], replicated, may hold values from 0 to 7, each once
- refresh: int32 [8], replicated, may hold values 0 or 1
Outputs:
- factor_new: float32 [8, 1024, 1024], P('mp', 'dp')
- roots_new: float32 [8, 1024, 1024], P('mp', 'dp')
- update: float32 [1, 16, 8192], replicated
Inputs may be any that keep to these rules, and one draw needn't show every extreme that they name: `owner_block_order`: a permutation: every block appears at exactly one owner position.
All inputs are finite; a program needn't handle non-finite values.
Results may differ from a plain program's by a relative error of at most 0.0003.
Values sent between devices are 32-bit elements; how exact they have to be, the bound alone decides.
A program may use at most 64 MiB of HBM per device.

v0:
```python
import jax
import jax.numpy as jnp
from jax import lax
from jax.sharding import PartitionSpec as P

D = 8192


DECAY = 0.75
DAMPING = 0.1
HIGH = lax.Precision.HIGHEST


def right_product(left_side, piece):
    return jnp.einsum(
        "brj,bjc->brc", left_side, piece, precision=HIGH, preferred_element_type=jnp.float32
    )


def body(
    acts,
    rank_space_gradient,
    running_factor_blocks,
    inverse_root_blocks,
    owner_block_order,
    refresh,
):
    owned_count = running_factor_blocks.shape[0]
    row_count = running_factor_blocks.shape[1]
    block_width = running_factor_blocks.shape[2]
    token_count = acts.shape[1]
    adapter_rank_width = rank_space_gradient.shape[2]
    layer_count = acts.shape[0]
    per_layer = D // block_width
    per_local = acts.shape[2] // block_width
    total_tokens = token_count * lax.axis_size("dp")
    n_data = lax.axis_size("dp")
    n_model = lax.axis_size("mp")
    selected_block = acts[0, :, 0:block_width]
    columns = [selected_block]
    local_gradient_rows = [
        jnp.einsum(
            "hc,hj->cj", selected_block, rank_space_gradient[0], preferred_element_type=jnp.float32
        )
    ]
    held_count = len(columns)
    selected_block = columns[0]
    pieces_list = jnp.einsum(
        "tc,tb->cb", selected_block, columns[0], preferred_element_type=jnp.float32
    )
    summed = lax.psum_scatter(pieces_list, "dp", scatter_dimension=0, tiled=True)
    grad_totals = lax.psum(jnp.stack(local_gradient_rows), "dp")
    routed_cov, routed_grad = (
        lax.all_gather(summed[None], "mp", axis=0, tiled=True),
        lax.all_gather(grad_totals[None], "mp", axis=0, tiled=True),
    )
    cov_all = routed_cov.reshape(n_model, row_count, held_count, block_width).transpose(0, 2, 1, 3)
    cov_all = cov_all.reshape(n_model * held_count, row_count, block_width)
    grad_all = routed_grad.reshape(n_model * held_count, block_width, adapter_rank_width)
    owned_blocks = lax.dynamic_slice_in_dim(
        owner_block_order, lax.axis_index("mp") * owned_count, owned_count, 0
    )
    block_id = owned_blocks[0]
    layer_number = block_id // per_layer
    inner = block_id % per_layer
    holder = inner // per_local * held_count + layer_number * per_local + inner % per_local
    cov_list = [lax.dynamic_index_in_dim(cov_all, holder, 0, keepdims=False)]
    grad_list = [lax.dynamic_index_in_dim(grad_all, holder, 0, keepdims=False)]
    flags = lax.dynamic_slice_in_dim(refresh, block_id, 1, 0)
    covariance = jnp.stack(cov_list) / total_tokens
    gradients = jnp.stack(grad_list)
    factor_new = DECAY * running_factor_blocks + (1.0 - DECAY) * covariance
    row_start = lax.axis_index("dp") * row_count
    row_ids = lax.broadcasted_iota(jnp.int32, (row_count, block_width), 0) + row_start
    col_ids = lax.broadcasted_iota(jnp.int32, (row_count, block_width), 1)
    eye_rows = (row_ids == col_ids).astype(jnp.float32)
    damped = factor_new + DAMPING * eye_rows[None]
    first_term = right_product(
        inverse_root_blocks, lax.all_gather(damped, "dp", axis=1, tiled=True)
    )
    second_term = right_product(
        first_term, lax.all_gather(inverse_root_blocks, "dp", axis=1, tiled=True)
    )
    third_term = right_product(
        second_term, lax.all_gather(inverse_root_blocks, "dp", axis=1, tiled=True)
    )
    conditioned = jnp.einsum(
        "brj,bjk->brk",
        inverse_root_blocks,
        gradients,
        precision=HIGH,
        preferred_element_type=jnp.float32,
    )
    stepped = 1.5 * inverse_root_blocks - 0.5 * third_term
    roots_new = jnp.where(flags[:, None, None] == 1, stepped, inverse_root_blocks)
    collected = lax.all_gather(conditioned, ("dp", "mp"), axis=1, tiled=True)
    arranged = collected.reshape(owned_count, n_data, n_model, row_count, adapter_rank_width)
    arranged = arranged.transpose(2, 0, 1, 3, 4).reshape(
        n_model * owned_count, n_data * row_count, adapter_rank_width
    )
    block_total = n_model * owned_count
    block_ids = lax.broadcasted_iota(jnp.int32, (block_total, block_total), 1)
    selector = (owner_block_order[:, None] == block_ids).astype(jnp.float32)
    ordered = jnp.einsum(
        "kb,kir->bir", selector, arranged, precision=HIGH, preferred_element_type=jnp.float32
    )
    update = ordered.reshape(layer_count, per_layer, block_width, adapter_rank_width).transpose(
        0, 3, 1, 2
    )
    update = update.reshape(layer_count, adapter_rank_width, per_layer * block_width)
    return (factor_new, roots_new, update)


def solution(mesh):
    return jax.shard_map(
        body,
        mesh=mesh,
        in_specs=(
            P(None, "dp", "mp"),
            P(None, "dp", None),
            P("mp", "dp", None),
            P("mp", "dp", None),
            P(),
            P(),
        ),
        out_specs=(P("mp", "dp", None), P("mp", "dp", None), P()),
        check_vma=False,
    )
```

profile of v0, /device:TPU:1, one launch (start us, length us, event | category | flops | bytes accessed | tf_op | source)
XLA Modules:
  0.0 1104.9 jit_solution(7352757172551622553)
XLA Ops:
  7.2 0.0 reduce-scatter.2.cloned.1.call-start
  7.2 15.1 %fusion.2 = f32[1024,1024]{1,0:T(8,128)} fusion(bf16[1,4096,1024]{2,1,0:T(8,128)(2,1)} %param.6), kind=kOutput, calls=%fused_computation.2 | convolution fusion | flops 8589934592 | bytes 12582912 | tf_op jit(solution)/shard_map/tc,tb->cb/dot_general | solution.py:48
  22.3 0.0 all-gather.11.cloned.1.call-start
  22.4 217.8 %reduce-scatter.2.cloned.1.call-done = f32[32,1024]{1,0:T(8,128)} async-done(((f32[1024,1024]{1,0:T(8,128)}), f32[32,1024]{1,0:T(8,128)}) %reduce-scatter.2.cloned.1.call-update) | async-done | bytes 131088 | tf_op jit(solution)/shard_map/reduce_scatter | solution.py:51
  240.3 0.0 all-reduce.2.cloned.1.call-start
  240.3 5.3 fusion.22
  245.6 0.0 all-gather.7.cloned.1.call-start
  245.7 0.7 dynamic_slice.14
  248.9 43.2 %all-gather.11.cloned.1.call-done = f32[256,1024]{1,0:T(8,128)} async-done(((f32[32,1024]{1,0:T(8,128)}), f32[256,1024]{1,0:T(8,128)}) %all-gather.11.cloned.1.call-update) | async-done | bytes 1048592 | tf_op jit(solution)/shard_map/all_gather | solution.py:54
  292.1 1.6 select_add_fusion
  293.8 0.0 all-gather.9.cloned.1.call-start
  293.8 0.5 all-gather.9.cloned.1.call-update
  295.6 0.7 dynamic_slice.16
  297.0 375.0 %all-reduce.2.cloned.1.call-done = f32[1,1,1024,16]{2,3,1,0:T(8,128)} async-done(((f32[1,1,1024,16]{2,3,1,0:T(8,128)}), f32[1,1,1024,16]{2,3,1,0:T(8,128)}) %all-reduce.2.cloned.1.call-update) | async-done | bytes 65552 | tf_op jit(solution)/shard_map/psum | solution.py:52
  671.9 25.9 %all_gather.19 = f32[8,1,1024,16]{2,3,1,0:T(8,128)S(1)} all-gather(f32[1,1,1024,16]{2,3,1,0:T(8,128)} %all-reduce.2.cloned.1.call-done), channel_id=1, replica_groups=mesh['dp'=32,'mp'=8] {'mp'}, dimensions={0}, use_global_device_ids=true | all-gather | bytes 589824 | tf_op jit(solution)/shard_map/all_gather | solution.py:55
  697.8 0.2 convolution_bitcast_fusion.1
  698.0 380.4 %all-gather.2 = f32[256,32,16]{1,2,0:T(8,128)S(1)} all-gather(f32[1,32,16]{1,2,0:T(8,128)S(1)} %convolution_bitcast_fusion.1), channel_id=3, replica_groups=mesh['dp'=32,'mp'=8] {'dp','mp'}, dimensions={0}, use_global_device_ids=true | all-gather | bytes 526336 | tf_op jit(solution)/shard_map/all_gather | solution.py:96
  1078.4 1.2 copy.12
  1079.6 1.0 reshape.82
  1080.6 0.4 convolution_bitcast_fusion
  1081.0 0.9 reshape.84
  1081.9 8.5 fusion.8
  1090.4 4.8 fusion.6
  1095.2 3.2 fusion.19
  (19 shorter events, 0.1 us)
Async XLA Ops:
  7.2 233.2 %copy-start = (bf16[1,4096,16]{1,2,0:T(8,128)(2,1)S(1)}, bf16[1,4096,16]{1,2,0:T(8,128)(2,1)}, u32[]{:S(2)}) copy-start(bf16[1,4096,16]{1,2,0:T(8,128)(2,1)} %param.7) | copy-start | bytes 393220
  7.2 233.0 %reduce-scatter.2.cloned.1.call-start = ((), (), s32[]{:S(2)}) async-start(), calls=%async_computation.1 | async-start | bytes 4325376 | tf_op jit(solution)/shard_map/reduce_scatter | solution.py:51
  22.3 269.8 %all-gather.11.cloned.1.call-start = ((), (), s32[]{:S(2)}) async-start(), calls=%async_computation.5 | async-start | bytes 1179648 | tf_op jit(solution)/shard_map/all_gather | solution.py:54
  240.2 5.4 copy-start.4
  240.2 51.9 %copy-start.3 = (f32[1,32,1024]{2,1,0:T(8,128)S(1)}, f32[1,32,1024]{2,1,0:T(8,128)}, u32[]{:S(2)}) copy-start(f32[1,32,1024]{2,1,0:T(8,128)} %param.8) | copy-start | bytes 393220
  240.3 55.4 %copy-start.5 = (s32[8]{0:T(128)S(1)}, s32[8]{0:T(128)}, u32[]{:S(2)}) copy-start(s32[8]{0:T(128)} %param.11) | copy-start | bytes 100
  240.3 457.5 %copy-start.2 = (f32[1,32,1024]{2,1,0:T(8,128)S(1)}, f32[1,32,1024]{2,1,0:T(8,128)}, u32[]{:S(2)}) copy-start(f32[1,32,1024]{2,1,0:T(8,128)} %param.9) | copy-start | bytes 393220
  240.3 431.6 %all-reduce.2.cloned.1.call-start = ((), (), s32[]{:S(2)}) async-start(), calls=%async_computation.4 | async-start | bytes 131072 | tf_op jit(solution)/shard_map/psum | solution.py:52
  245.6 836.2 %all-gather.7.cloned.1.call-start = ((), (), s32[]{:S(2)}) async-start(), calls=%async_computation.2 | async-start | bytes 4325376 | tf_op jit(solution)/shard_map/all_gather | solution.py:79
  293.8 796.6 %all-gather.9.cloned.1.call-start = ((), (), s32[]{:S(2)}) async-start(), calls=%async_computation.3 | async-start | bytes 4325376 | tf_op jit(solution)/shard_map/all_gather | solution.py:82
  1090.3 4.9 copy-start.1
Sparse Core Ops, SparseCore 0:
  22.5 217.7 reduce-scatter.1
  242.0 50.0 all-gather.10
  295.3 376.5 all-reduce.1
  676.3 118.1 all-gather.6
  798.3 108.5 all-gather.8
where the time goes:
time: 1110 us; the launch traced here: 1100 us
  waiting for transfers between devices  637 us (57%)
  blocking collectives  406 us (37%)
  matrix products  37.3 us (3%)
  between operations  18.4 us (2%)
    all_gather x1, blocking collectives, body(): collected = lax.all_gather(conditioned, ('dp', 'mp'), axis=1, tiled=True)  380 us
    psum x1, waiting for transfers between devices, body(): grad_totals = lax.psum(jnp.stack(local_gradient_rows), 'dp')  375 us
    reduce_scatter x1, waiting for transfers between devices, body(): lax.psum_scatter(pieces_list, 'dp', scatter_dimension=0, tiled=True)  218 us
    all_gather x1, waiting for transfers between devices, body(): lax.all_gather(summed[None], 'mp', axis=0, tiled=True)  43.2 us
    all_gather x1, blocking collectives, body(): lax.all_gather(grad_totals[None], 'mp', axis=0, tiled=True)  25.9 us
  transfers between devices with their start and end apart: 5, of which 3 were waited for; matrix products, arithmetic and copies ran while one was open for 2% of the time, Pallas kernels for 0%

commit v1 on v0

v1 whole, which is shorter than its diff:
```python
import functools

import jax
import jax.numpy as jnp
from jax import lax
from jax.experimental import pallas as pl
from jax.experimental.pallas import tpu as pltpu
from jax.sharding import PartitionSpec as P

D = 8192
DECAY = 0.75
DAMPING = 0.1
MESH = pl.DeviceIdType.MESH
NN = (((1,), (0,)), ((), ()))
NT = (((1,), (1,)), ((), ()))
TN = (((0,), (0,)), ((), ()))
SEMS = 192
F32 = jnp.float32
BF16 = jnp.bfloat16

GROUPS = ((4, 5, 6, 7), (0, 1, 2, 3))


def width(p):
    return 640 if p <= 4 else 512


def dot(a, b, dims=NN):
    return lax.dot_general(a, b, dims, preferred_element_type=F32)


def split(v):
    high = v.astype(BF16)
    return high, (v - high.astype(F32)).astype(BF16)


def dot_split(stacked, high, low, dims=NN):
    rows = stacked.shape[0] // 2
    both = dot(stacked, high, dims)
    return both[:rows] + both[rows:] + dot(stacked[:rows], low, dims)


def kernel(
    tokens,
    order, refresh, x_hbm, g_hbm, r_hbm, y_hbm,
    fo, ro, uo,
    x, g, rsh, yb, yh, yl, ystk, pan, r1, s1, r2, zb0, zb1, sibs, sibr, cag,
    rcol, vs, vr, f, tb, ub, lsem, ssem, rsem,
):
    scale = (1.0 - DECAY) / tokens
    zb = (zb0, zb1)
    dp = lax.axis_index("dp")
    mp = lax.axis_index("mp")
    cy, czh, cx = dp // 8, (dp // 4) % 2, dp % 4
    czl, cc = mp // 2, mp % 2
    cz = czh * 4 + czl

    def dev(y, zh, xx, zl, c):
        return {"dp": (y * 2 + zh) * 4 + xx, "mp": zl * 2 + c}

    def zdev(d):
        w = (cz + d) % 8
        return dev(cy, w // 4, cx, w % 4, cc)

    px = {d: dev(cy, czh, (cx + d) % 4, czl, cc) for d in (1, 2, 3)}
    py = {d: dev((cy + d) % 4, czh, cx, czl, cc) for d in (1, 2, 3)}
    pa = {
        (dz, dx): dev(cy, (czh + dz) % 2, (cx + dx) % 4, czl, cc)
        for dz in (0, 1) for dx in (0, 1, 2, 3) if dz or dx
    }
    z_up, z_down = zdev(1), zdev(7)
    sibling = dev(cy, czh, cx, czl, 1 - cc)
    AX = {"x": (cx, px), "y": (cy, py)}

    count = [0]
    sent = []

    def send(src, dst, target):
        i = count[0]
        count[0] += 1
        copy = pltpu.make_async_remote_copy(
            src_ref=src, dst_ref=dst, send_sem=ssem.at[i], recv_sem=rsem.at[i],
            device_id=target, device_id_type=MESH,
        )
        copy.start()
        sent.append(copy)
        return copy

    def arrive(copies):
        for c in copies:
            c.wait_recv()

    own_y = yb.at[cy, czh, cx]
    load_y = pltpu.make_async_copy(y_hbm.at[0], own_y, lsem.at[0])
    load_r = pltpu.make_async_copy(r_hbm.at[0], rsh, lsem.at[1])
    load_y.start()
    load_r.start()
    nk = 4
    depth = x.shape[0] // nk
    load_x = [
        pltpu.make_async_copy(x_hbm.at[0, pl.ds(i * depth, depth)], x.at[pl.ds(i * depth, depth)], lsem.at[3 + i])
        for i in range(nk)
    ]
    for c in load_x:
        c.start()
    load_g = pltpu.make_async_copy(g_hbm, g, lsem.at[2])
    load_g.start()

    barrier = pltpu.get_barrier_semaphore()
    peers = list(pa.values()) + list(py.values()) + [z_up, z_down, sibling]
    for peer in peers:
        pl.semaphore_signal(barrier, inc=1, device_id=peer, device_id_type=MESH)
    pl.semaphore_wait(barrier, len(peers))

    def y_first(h):
        a = [send(yb.at[cy, h, cx, pl.ds(0, 16)], yb.at[cy, h, cx, pl.ds(0, 16)], px[d]) for d in (1, 2, 3)]
        b = [send(yb.at[cy, h, cx, pl.ds(16, 16)], yb.at[cy, h, cx, pl.ds(16, 16)], py[d]) for d in (1, 2, 3)]
        return a + b

    def y_second(h):
        a = [send(yb.at[cy, h, :, pl.ds(0, 16)], yb.at[cy, h, :, pl.ds(0, 16)], py[d]) for d in (1, 2, 3)]
        b = [send(yb.at[:, h, cx, pl.ds(16, 16)], yb.at[:, h, cx, pl.ds(16, 16)], px[d]) for d in (1, 2, 3)]
        return a + b

    my_j = czh * 4 + cx
    load_y.wait()
    y_z = send(own_y, own_y, pa[(1, 0)])
    y_own1 = y_first(czh)
    load_r.wait()
    r_a2a = []
    for (dz, dx), peer in pa.items():
        j = ((czh + dz) % 2) * 4 + (cx + dx) % 4
        r_a2a.append(
            send(rsh.at[:, pl.ds(pl.multiple_of(j * 128, 128), 128)], rcol.at[cy, my_j], peer)
        )
    rcol[cy, my_j] = rsh[:, pl.ds(pl.multiple_of(my_j * 128, 128), 128)]

    yr = yb[cy, czh, cx]
    yrh, yrl = split(yr)
    ystk[0:32, 0:1024] = yrh
    ystk[0:32, 1024:1536] = yrh[:, :512]
    ystk[32:64, 0:1024] = yrl
    ystk[32:64, 1024:1536] = yrl[:, :512]

    def gemm(i, k0, kn, first):
        lo = 256 * i
        n = 768 if i < 2 else 640
        segs = [(lo, n, 0)] if lo + n <= 1024 else [(lo, 1024 - lo, 0), (0, lo + n - 1024, 1024 - lo)]
        for start, w, at in segs:
            v = dot(x[k0:k0 + kn, lo:lo + 256], x[k0:k0 + kn, start:start + w], TN)
            for half in (0, 1):
                p = 2 * i + half
                cols = 640 if p < 4 else 512
                b0, b1 = max(at, 128 * half), min(at + w, 128 * half + cols)
                if b1 <= b0:
                    continue
                part = v[128 * half:128 * half + 128, b0 - at:b1 - at]
                c0 = b0 - 128 * half
                if first:
                    pan[p, :, c0:c0 + b1 - b0] = part
                else:
                    pan[p, :, c0:c0 + b1 - b0] += part

    ax1 = {p: AX["x" if p % 2 == 0 else "y"] for p in range(8)}
    ax2 = {p: AX["y" if p % 2 == 0 else "x"] for p in range(8)}

    def rs_first(p):
        a, peer = ax1[p]
        w = width(p)
        return [
            send(
                pan.at[p, pl.ds(pl.multiple_of(((a + d) % 4) * 32, 32), 32), pl.ds(0, w)],
                r1.at[p, d - 1, :, pl.ds(0, w)], peer[d],
            )
            for d in (1, 2, 3)
        ]

    def rs_second(p, copies):
        arrive(copies)
        a, _ = ax1[p]
        b, peer = ax2[p]
        w = width(p)
        s1[p, :, :w] = (
            pan[p, pl.ds(pl.multiple_of(a * 32, 32), 32), :w] + r1[p, 0, :, :w] + r1[p, 1, :, :w] + r1[p, 2, :, :w]
        )
        return [
            send(
                s1.at[p, pl.ds(pl.multiple_of(((b + d) % 4) * 8, 8), 8), pl.ds(0, w)],
                r2.at[p, d - 1, :, pl.ds(0, w)], peer[d],
            )
            for d in (1, 2, 3)
        ]

    def rs_end(p, copies):
        arrive(copies)
        b, _ = ax2[p]
        w = width(p)
        gi = 0 if p >= 4 else 1
        i = p % 4
        zb[gi][cz, 8 * i:8 * i + 8, :w] = (
            s1[p, pl.ds(pl.multiple_of(b * 8, 8), 8), :w] + r2[p, 0, :, :w] + r2[p, 1, :, :w] + r2[p, 2, :, :w]
        )
        if w < 640:
            zb[gi][cz, 8 * i:8 * i + 8, w:640] = jnp.zeros((8, 640 - w), F32)

    def z_step(gi, s):
        up, down = (cz - s) % 8, (cz + s) % 8
        if s < 3:
            u, v = zb[gi].at[up], zb[gi].at[down]
        else:
            u, v = zb[gi].at[up, pl.ds(0, 16)], zb[gi].at[down, pl.ds(16, 16)]
        return [send(u, u, z_up), send(v, v, z_down)]

    b_mine = order[2 * czl + cc]
    b_other = order[2 * czl + 1 - cc]

    def picked(gi, b):
        return zb[gi][b // 2] + zb[gi][b // 2 + 4]

    def to_sibling(gi):
        sibs[gi] = jnp.where(b_other % 2 == cc, picked(gi, b_other), 0.0)
        return [send(sibs.at[gi], sibr.at[gi], sibling)]

    def take(gi):
        v = jnp.where(b_mine % 2 == cc, picked(gi, b_mine), sibr[gi])
        for i, p in enumerate(GROUPS[gi]):
            a, _ = ax1[p]
            b, _ = ax2[p]
            w = width(p)
            cag[p, pl.ds(pl.multiple_of(a * 32 + b * 8, 8), 8), :w] = v[8 * i:8 * i + 8, :w]

    def ag_first(p):
        a, _ = ax1[p]
        b, peer = ax2[p]
        ref = cag.at[p, pl.ds(pl.multiple_of(a * 32 + b * 8, 8), 8), pl.ds(0, width(p))]
        return [send(ref, ref, peer[d]) for d in (1, 2, 3)]

    def ag_second(p, copies):
        arrive(copies)
        a, peer = ax1[p]
        ref = cag.at[p, pl.ds(pl.multiple_of(a * 32, 32), 32), pl.ds(0, width(p))]
        return [send(ref, ref, peer[d]) for d in (1, 2, 3)]

    c1, c2 = {}, {}
    for k in range(nk):
        load_x[k].wait()
        gemm(2, k * depth, depth, k == 0)
    load_g.wait()
    grads = dot(g[...], x[...])
    for j in range(8):
        pan[4, 16 * j:16 * j + 16, 512:640] = grads[:, 128 * j:128 * j + 128]
    c1[4], c1[5] = rs_first(4), rs_first(5)
    y_z.wait_recv()
    y_oth1 = y_first(1 - czh)
    gemm(3, 0, x.shape[0], True)
    c1[6], c1[7] = rs_first(6), rs_first(7)
    c2[4], c2[5] = rs_second(4, c1[4]), rs_second(5, c1[5])
    arrive(r_a2a)
    r_y = [send(rcol.at[cy], rcol.at[cy], py[d]) for d in (1, 2, 3)]
    gemm(0, 0, x.shape[0], True)
    c1[0], c1[1] = rs_first(0), rs_first(1)
    c2[6], c2[7] = rs_second(6, c1[6]), rs_second(7, c1[7])
    gemm(1, 0, x.shape[0], True)
    c1[2], c1[3] = rs_first(2), rs_first(3)
    arrive(y_own1)
    y_own2 = y_second(czh)
    c2[0], c2[1] = rs_second(0, c1[0]), rs_second(1, c1[1])
    for p in GROUPS[0]:
        rs_end(p, c2[p])
    za = z_step(0, 0)
    c2[2], c2[3] = rs_second(2, c1[2]), rs_second(3, c1[3])
    arrive(y_oth1)
    y_oth2 = y_second(1 - czh)
    for p in GROUPS[1]:
        rs_end(p, c2[p])
    zc = z_step(1, 0)
    for s in (1, 2, 3):
        arrive(za)
        za = z_step(0, s)
        arrive(zc)
        zc = z_step(1, s)
    arrive(za)
    sa = to_sibling(0)
    arrive(zc)
    sb = to_sibling(1)
    arrive(sa)
    take(0)
    g1 = {p: ag_first(p) for p in GROUPS[0]}
    arrive(sb)
    take(1)
    g1.update({p: ag_first(p) for p in GROUPS[1]})
    g2 = {p: ag_second(p, g1[p]) for p in GROUPS[0] + GROUPS[1]}

    arrive(y_own2)
    arrive(y_oth2)

    def convert(i, carry):
        v = yb[i // 8, (i // 4) % 2, i % 4]
        h, l = split(v)
        at = pl.ds(pl.multiple_of(i * 32, 32), 32)
        yh[at] = h
        yl[at] = l
        return carry

    lax.fori_loop(0, 32, convert, 0)
    arrive(r_y)
    n = 1024
    eye = (
        lax.broadcasted_iota(jnp.int32, (n, 128), 0) == lax.broadcasted_iota(jnp.int32, (n, 128), 1) + my_j * 128
    )
    rh, rl = split(DECAY * rcol[...].reshape(n, 128) + jnp.where(eye, DAMPING, 0.0))
    rows_i = pl.ds(pl.multiple_of(cy * 256, 256), 256)
    v = dot(yh[rows_i], rh) + dot(yl[rows_i], rh) + dot(yh[rows_i], rl)
    vs[...] = v.reshape(8, 32, 128)
    v_a2a = []
    for (dz, dx), peer in pa.items():
        j = ((czh + dz) % 2) * 4 + (cx + dx) % 4
        v_a2a.append(send(vs.at[j], vr.at[my_j], peer))
    vr[my_j] = vs[my_j]

    arrive(g2[4])
    pr = pl.ds(pl.multiple_of((2 * cy + czh) * 128, 128), 128)
    gk = jnp.concatenate([cag[4, 16 * j:16 * j + 16, 512:640] for j in range(8)], axis=1)
    gh, gl = split(gk)
    ub[cc, cz, cy] = dot_split(jnp.concatenate([gh, gl], axis=0), yh[pr], yl[pr], NT)
    u1 = [send(ub.at[cc, cz, cy], ub.at[cc, cz, cy], py[d]) for d in (1, 2, 3)]

    arrive(v_a2a)
    for j in range(8):
        f[:, 128 * j:128 * j + 128] = vr[j]

    def accumulate(p):
        nb = 5 if p < 4 else 4
        ch, cl = split(cag[p, :, :128 * nb] * scale)
        out = dot_split(ystk[:, 128 * p:128 * p + 128], ch, cl)
        for o in range(nb):
            j = (p + o) % 8
            f[:, 128 * j:128 * j + 128] += out[:, 128 * o:128 * o + 128]
        f[:, 128 * p:128 * p + 128] += dot_split(
            ystk[:, 128 * (p + 1):128 * (p + nb)], ch[:, 128:], cl[:, 128:], NT
        )

    def u_step(s):
        up, down = (cz - s) % 8, (cz + s) % 8
        if s < 3:
            u, w = ub.at[cc, up], ub.at[cc, down]
        else:
            u, w = ub.at[cc, up, pl.ds(0, 2)], ub.at[cc, down, pl.ds(2, 2)]
        return [send(u, u, z_up), send(w, w, z_down)]

    accumulate(4)
    arrive(u1)
    u2 = u_step(0)
    for s, p in ((1, 5), (2, 6), (3, 7)):
        arrive(g2[p])
        accumulate(p)
        arrive(u2)
        u2 = u_step(s)
    arrive(g2[0])
    accumulate(0)
    arrive(u2)
    u3 = send(ub.at[cc], ub.at[cc], sibling)
    for p in (1, 2, 3):
        arrive(g2[p])
        accumulate(p)

    def times_root(m):
        mh, ml = split(m)
        return dot_split(jnp.concatenate([mh, ml], axis=0), yh[...], yl[...])

    third = times_root(times_root(f[...]))
    yr = yb[cy, czh, cx]
    ro[0] = jnp.where(refresh[b_mine] == 1, 1.5 * yr - 0.5 * third, yr)

    panel = 2 * cy + czh
    rows_x = pl.ds(pl.multiple_of(cx * 32, 32), 32)

    def turned(block):
        tb[...] = block.T
        return tb[rows_x, :]

    for o in range(8):
        j = (panel + o) % 8
        if o < 4:
            c = cag[panel, rows_x, 128 * o:128 * o + 128]
        elif o == 4:
            q = panel % 4
            c = jnp.where(panel < 4, cag[q, rows_x, 512:640], turned(cag[q, :, 512:640]))
        else:
            c = turned(cag[j, :, 128 * (8 - o):128 * (8 - o) + 128])
        at = pl.ds(pl.multiple_of(j * 128, 128), 128)
        fo[0, :, at] = DECAY * rsh[:, at] + scale * c

    u3.wait_recv()
    for b in range(8):
        k = jnp.int32(0)
        for q in range(8):
            k = jnp.where(order[q] == b, q, k)
        for q in range(8):
            uo[0, :, 1024 * b + 128 * q:1024 * b + 128 * q + 128] = ub[k % 2, (q % 2) * 4 + k // 2, q // 2]

    for c in sent:
        c.wait_send()


def body(acts, rank_space_gradient, running_factor_blocks, inverse_root_blocks, owner_block_order, refresh):
    tokens_here = acts.shape[1]
    tokens = tokens_here * lax.axis_size("dp")
    hbm = pl.BlockSpec(memory_space=pl.ANY)
    smem = pl.BlockSpec(memory_space=pltpu.SMEM)
    vmem = pl.BlockSpec(memory_space=pltpu.VMEM)
    return pl.pallas_call(
        functools.partial(kernel, tokens),
        out_shape=(
            jax.ShapeDtypeStruct((1, 32, 1024), F32),
            jax.ShapeDtypeStruct((1, 32, 1024), F32),
            jax.ShapeDtypeStruct((1, 16, D), F32),
        ),
        in_specs=[smem, smem, hbm, hbm, hbm, hbm],
        out_specs=(vmem, vmem, vmem),
        scratch_shapes=[
            pltpu.VMEM((tokens_here, 1024), BF16),
            pltpu.VMEM((16, tokens_here), BF16),
            pltpu.VMEM((32, 1024), F32),
            pltpu.VMEM((4, 2, 4, 32, 1024), F32),
            pltpu.VMEM((1024, 1024), BF16),
            pltpu.VMEM((1024, 1024), BF16),
            pltpu.VMEM((64, 1536), BF16),
            pltpu.VMEM((8, 128, 640), F32),
            pltpu.VMEM((8, 3, 32, 640), F32),
            pltpu.VMEM((8, 32, 640), F32),
            pltpu.VMEM((8, 3, 8, 640), F32),
            pltpu.VMEM((8, 32, 640), F32),
            pltpu.VMEM((8, 32, 640), F32),
            pltpu.VMEM((2, 32, 640), F32),
            pltpu.VMEM((2, 32, 640), F32),
            pltpu.VMEM((8, 128, 640), F32),
            pltpu.VMEM((4, 8, 32, 128), F32),
            pltpu.VMEM((8, 32, 128), F32),
            pltpu.VMEM((8, 32, 128), F32),
            pltpu.VMEM((32, 1024), F32),
            pltpu.VMEM((128, 128), F32),
            pltpu.VMEM((2, 8, 4, 16, 128), F32),
            pltpu.SemaphoreType.DMA((8,)),
            pltpu.SemaphoreType.DMA((SEMS,)),
            pltpu.SemaphoreType.DMA((SEMS,)),
        ],
        compiler_params=pltpu.CompilerParams(
            collective_id=0, has_side_effects=True, vmem_limit_bytes=56 * 1024 * 1024
        ),
        cost_estimate=pl.CostEstimate(flops=8_000_000_000, bytes_accessed=12_000_000, transcendentals=0),
        name="kfac_step",
    )(
        owner_block_order,
        refresh,
        acts,
        jnp.swapaxes(rank_space_gradient[0], 0, 1),
        running_factor_blocks,
        inverse_root_blocks,
    )


def solution(mesh):
    return jax.shard_map(
        body,
        mesh=mesh,
        in_specs=(
            P(None, "dp", "mp"),
            P(None, "dp", None),
            P("mp", "dp", None),
            P("mp", "dp", None),
            P(),
            P(),
        ),
        out_specs=(P("mp", "dp", None), P("mp", "dp", None), P()),
        check_vma=False,
    )
```

time: 1110 us -> 124 us (0.11)
  waiting for transfers between devices: 637 us -> 0 us
  blocking collectives: 406 us -> 0 us
  Pallas kernels: 0 us -> 116 us
  matrix products: 37.3 us -> 0 us
  between operations: 18.4 us -> 0.64 us
    all_gather x2 -> x0, blocking collectives: 406 us -> none  [the longest x1 380 us: body(): collected = lax.all_gather(conditioned, ('dp', 'mp'), axis=1, tiled=True)]
    psum x1 -> x0, waiting for transfers between devices: 375 us -> none  [body(): grad_totals = lax.psum(jnp.stack(local_gradient_rows), 'dp')]
    reduce_scatter x1 -> x0, waiting for transfers between devices: 218 us -> none  [body(): lax.psum_scatter(pieces_list, 'dp', scatter_dimension=0, tiled=True)]
    pallas_call x0 -> x1, Pallas kernels: none -> 116 us  [body(): pl.pallas_call(functools.partial(kernel, tokens), out_shape=(jax.ShapeDty...]
    all_gather x3 -> x0, waiting for transfers between devices: 43.3 us -> none  [the longest x1 43.2 us: body(): lax.all_gather(summed[None], 'mp', axis=0, tiled=True)]
    dot_general x7 -> x0, matrix products: 37.3 us -> none  [the longest x3 16.5 us: right_product(): jnp.einsum('brj,bjc->brc', left_side, piece, precision=HIGH, preferred_el...]
  transfers between devices with their start and end apart: 5 -> 0, of which waited for: 3 -> 0; matrix products, arithmetic and copies ran while one was open for 2% -> 0% of each run, Pallas kernels for 0% -> 0%
where the time goes in v1:
time: 124 us; the launch traced here: 122 us
  Pallas kernels  116 us (94%)
  local copies, waits for them, and re-layouts  5 us (4%)
    pallas_call x1, Pallas kernels, body(): pl.pallas_call(functools.partial(kernel, tokens), out_shape=(jax.ShapeDty...  116 us
    unnamed x3, local copies, waits for them, and re-layouts  5 us

profile of v1, /device:TPU:1, one launch (start us, length us, event | category | flops | bytes accessed | tf_op | source)
XLA Modules:
  0.0 121.8 jit_solution(2160462226360420817)
XLA Ops:
  0.6 116.2 %kfac_step.1 = (f32[1,32,1024]{2,1,0:T(8,128)}, f32[1,32,1024]{2,1,0:T(8,128)}, f32[1,16,8192]{2,1,0:T(8,128)}) custom-call(s32[8]{0:T(128)} %order.1, s32[8]{0:T(128)} %refresh.1, bf16[1,4096,1024]{2,1,0:T(8,128)(2,1)} %x_hbm.1, bf16[16,4096]{1,0:T(8,128)(2,1)} %bitcast.3, f32[1,32,1024]{2,1,0:T(8,128)} %r_hbm.1, f32[1,32,1024]{2,1,0:T(8,128)} %y_hbm.1), custom_call_target="tpu_custom_call" | custom-call | flops 8000000000 | bytes 12000000 | tf_op jit(solution)/shard_map/kfac_step/pallas_call | solution.py:412
  116.8 1.6 %copy.12 = f32[1,32,1024]{2,1,0:T(8,128)} copy(f32[1,32,1024]{2,1,0:T(8,128)} %get-tuple-element.6) | data formatting | bytes 262144
  118.4 1.6 %copy.13 = f32[1,32,1024]{2,1,0:T(8,128)} copy(f32[1,32,1024]{2,1,0:T(8,128)} %get-tuple-element.7) | data formatting | bytes 262144
  120.0 1.9 %copy.14 = f32[1,16,8192]{2,1,0:T(8,128)} copy(f32[1,16,8192]{2,1,0:T(8,128)} %get-tuple-element.8) | data formatting | bytes 1048576

commit v2 on v1

--- a/solution.py
+++ b/solution.py
@@ -14,7 +14,7 @@
 NN = (((1,), (0,)), ((), ()))
 NT = (((1,), (1,)), ((), ()))
 TN = (((0,), (0,)), ((), ()))
-SEMS = 192
+SEMS = 200
 F32 = jnp.float32
 BF16 = jnp.bfloat16
 
@@ -44,7 +44,7 @@
     tokens,
     order, refresh, x_hbm, g_hbm, r_hbm, y_hbm,
     fo, ro, uo,
-    x, g, rsh, yb, yh, yl, ystk, pan, r1, s1, r2, zb0, zb1, sibs, sibr, cag,
+    x, g, rsh, yb, yh, yl, ystk, pan, r0, t1, r1, s1, r2, zb0, zb1, sibs, sibr, cag,
     rcol, vs, vr, f, tb, ub, lsem, ssem, rsem,
 ):
     scale = (1.0 - DECAY) / tokens
@@ -68,7 +68,8 @@
         (dz, dx): dev(cy, (czh + dz) % 2, (cx + dx) % 4, czl, cc)
         for dz in (0, 1) for dx in (0, 1, 2, 3) if dz or dx
     }
-    z_up, z_down = zdev(1), zdev(7)
+    pz = {d: zdev(d) for d in range(1, 8)}
+    z_up, z_down = pz[1], pz[7]
     sibling = dev(cy, czh, cx, czl, 1 - cc)
     AX = {"x": (cx, px), "y": (cy, py)}
 
@@ -107,7 +108,7 @@
     load_g.start()
 
     barrier = pltpu.get_barrier_semaphore()
-    peers = list(pa.values()) + list(py.values()) + [z_up, z_down, sibling]
+    peers = list(pa.values()) + list(py.values()) + [pz[d] for d in (1, 2, 3, 5, 6, 7)] + [sibling]
     for peer in peers:
         pl.semaphore_signal(barrier, inc=1, device_id=peer, device_id_type=MESH)
     pl.semaphore_wait(barrier, len(peers))
@@ -118,9 +119,20 @@
         return a + b
 
     def y_second(h):
-        a = [send(yb.at[cy, h, :, pl.ds(0, 16)], yb.at[cy, h, :, pl.ds(0, 16)], py[d]) for d in (1, 2, 3)]
-        b = [send(yb.at[:, h, cx, pl.ds(16, 16)], yb.at[:, h, cx, pl.ds(16, 16)], px[d]) for d in (1, 2, 3)]
+        a = [send(yb.at[cy, h, :, pl.ds(0, 16)], yb.at[cy, h, :, pl.ds(0, 16)], py[d]) for d in (1, 3)]
+        b = [send(yb.at[:, h, cx, pl.ds(16, 16)], yb.at[:, h, cx, pl.ds(16, 16)], px[d]) for d in (1, 3)]
         return a + b
+
+    def y_third(h, copies):
+        arrive(copies)
+        out = []
+        for d, at in ((3, 0), (1, 8)):
+            ya, xa = (cy + d) % 4, (cx + d) % 4
+            ref = yb.at[ya, h, :, pl.ds(at, 8)]
+            out.append(send(ref, ref, py[4 - d]))
+            ref = yb.at[:, h, xa, pl.ds(16 + at, 8)]
+            out.append(send(ref, ref, px[4 - d]))
+        return out
 
     my_j = czh * 4 + cx
     load_y.wait()
@@ -164,25 +176,33 @@
     ax1 = {p: AX["x" if p % 2 == 0 else "y"] for p in range(8)}
     ax2 = {p: AX["y" if p % 2 == 0 else "x"] for p in range(8)}
 
+    def quarter(a, at=0, rows=32):
+        return pl.ds(pl.multiple_of((a % 4) * 32 + at, 8), rows)
+
     def rs_first(p):
         a, peer = ax1[p]
+        w = pl.ds(0, width(p))
+        return [
+            send(pan.at[p, quarter(a + 2, 16 * i, 16), w], r0.at[p, i, :, w], peer[d]) for i, d in ((0, 1), (1, 3))
+        ]
+
+    def rs_mid(p, copies):
+        arrive(copies)
+        a, peer = ax1[p]
         w = width(p)
-        return [
-            send(
-                pan.at[p, pl.ds(pl.multiple_of(((a + d) % 4) * 32, 32), 32), pl.ds(0, w)],
-                r1.at[p, d - 1, :, pl.ds(0, w)], peer[d],
-            )
-            for d in (1, 2, 3)
-        ]
+        out = []
+        for i, d in ((0, 1), (1, 3)):
+            t1[p, i, 16 * i:16 * i + 16, :w] = pan[p, quarter(a + d, 16 * i, 16), :w] + r0[p, i, :, :w]
+            t1[p, i, 16 - 16 * i:32 - 16 * i, :w] = pan[p, quarter(a + d, 16 - 16 * i, 16), :w]
+            out.append(send(t1.at[p, i, :, pl.ds(0, w)], r1.at[p, i, :, pl.ds(0, w)], peer[d]))
+        return out
 
     def rs_second(p, copies):
         arrive(copies)
         a, _ = ax1[p]
         b, peer = ax2[p]
         w = width(p)
-        s1[p, :, :w] = (
-            pan[p, pl.ds(pl.multiple_of(a * 32, 32), 32), :w] + r1[p, 0, :, :w] + r1[p, 1, :, :w] + r1[p, 2, :, :w]
-        )
+        s1[p, :, :w] = pan[p, quarter(a), :w] + r1[p, 0, :, :w] + r1[p, 1, :, :w]
         return [
             send(
                 s1.at[p, pl.ds(pl.multiple_of(((b + d) % 4) * 8, 8), 8), pl.ds(0, w)],
@@ -238,10 +258,20 @@
     def ag_second(p, copies):
         arrive(copies)
         a, peer = ax1[p]
-        ref = cag.at[p, pl.ds(pl.multiple_of(a * 32, 32), 32), pl.ds(0, width(p))]
-        return [send(ref, ref, peer[d]) for d in (1, 2, 3)]
-
-    c1, c2 = {}, {}
+        ref = cag.at[p, quarter(a), pl.ds(0, width(p))]
+        return [send(ref, ref, peer[d]) for d in (1, 3)]
+
+    def ag_third(p, copies):
+        arrive(copies)
+        a, peer = ax1[p]
+        out = []
+        for d, at in ((3, 0), (1, 16)):
+            ref = cag.at[p, quarter(a + d, at, 16), pl.ds(0, width(p))]
+            out.append(send(ref, ref, peer[4 - d]))
+        return out
+
+    c1, cm, c2, g1, g2, g3 = {}, {}, {}, {}, {}, {}
+    ga, gb = GROUPS
     for k in range(nk):
         load_x[k].wait()
         gemm(2, k * depth, depth, k == 0)
@@ -249,50 +279,110 @@
     grads = dot(g[...], x[...])
     for j in range(8):
         pan[4, 16 * j:16 * j + 16, 512:640] = grads[:, 128 * j:128 * j + 128]
-    c1[4], c1[5] = rs_first(4), rs_first(5)
+    for p in (4, 5):
+        c1[p] = rs_first(p)
     y_z.wait_recv()
     y_oth1 = y_first(1 - czh)
     gemm(3, 0, x.shape[0], True)
-    c1[6], c1[7] = rs_first(6), rs_first(7)
-    c2[4], c2[5] = rs_second(4, c1[4]), rs_second(5, c1[5])
-    arrive(r_a2a)
-    r_y = [send(rcol.at[cy], rcol.at[cy], py[d]) for d in (1, 2, 3)]
+    for p in (6, 7):
+        c1[p] = rs_first(p)
+    for p in (4, 5):
+        cm[p] = rs_mid(p, c1[p])
     gemm(0, 0, x.shape[0], True)
-    c1[0], c1[1] = rs_first(0), rs_first(1)
-    c2[6], c2[7] = rs_second(6, c1[6]), rs_second(7, c1[7])
+    for p in (0, 1):
+        c1[p] = rs_first(p)
+    for p in (6, 7):
+        cm[p] = rs_mid(p, c1[p])
+    for p in (4, 5):
+        c2[p] = rs_second(p, cm[p])
     gemm(1, 0, x.shape[0], True)
-    c1[2], c1[3] = rs_first(2), rs_first(3)
+    for p in (2, 3):
+        c1[p] = rs_first(p)
+    for p in (0, 1):
+        cm[p] = rs_mid(p, c1[p])
+    for p in (6, 7):
+        c2[p] = rs_second(p, cm[p])
+    for p in ga:
+        rs_end(p, c2[p])
+    za = z_step(0, 0)
+    for p in (2, 3):
+        cm[p] = rs_mid(p, c1[p])
     arrive(y_own1)
     y_own2 = y_second(czh)
-    c2[0], c2[1] = rs_second(0, c1[0]), rs_second(1, c1[1])
-    for p in GROUPS[0]:
+    arrive(za)
+    za = z_step(0, 1)
+    for p in (0, 1):
+        c2[p] = rs_second(p, cm[p])
+    arrive(za)
+    za = z_step(0, 2)
+    for p in (2, 3):
+        c2[p] = rs_second(p, cm[p])
+    for p in gb:
         rs_end(p, c2[p])
-    za = z_step(0, 0)
-    c2[2], c2[3] = rs_second(2, c1[2]), rs_second(3, c1[3])
+    zc = z_step(1, 0)
+    arrive(za)
+    za = z_step(0, 3)
+    y_own3 = y_third(czh, y_own2)
     arrive(y_oth1)
     y_oth2 = y_second(1 - czh)
-    for p in GROUPS[1]:
-        rs_end(p, c2[p])
-    zc = z_step(1, 0)
-    for s in (1, 2, 3):
-        arrive(za)
-        za = z_step(0, s)
-        arrive(zc)
-        zc = z_step(1, s)
+    arrive(zc)
+    zc = z_step(1, 1)
     arrive(za)
     sa = to_sibling(0)
     arrive(zc)
-    sb = to_sibling(1)
+    zc = z_step(1, 2)
     arrive(sa)
     take(0)
-    g1 = {p: ag_first(p) for p in GROUPS[0]}
+    for p in ga:
+        g1[p] = ag_first(p)
+    arrive(r_a2a)
+    r_y = [send(rcol.at[cy], rcol.at[cy], py[d]) for d in (1, 2, 3)]
+    arrive(zc)
+    zc = z_step(1, 3)
+    for p in ga:
+        g2[p] = ag_second(p, g1[p])
+    arrive(zc)
+    sb = to_sibling(1)
+    for p in ga:
+        g3[p] = ag_third(p, g2[p])
     arrive(sb)
     take(1)
-    g1.update({p: ag_first(p) for p in GROUPS[1]})
-    g2 = {p: ag_second(p, g1[p]) for p in GROUPS[0] + GROUPS[1]}
-
-    arrive(y_own2)
-    arrive(y_oth2)
+    for p in gb:
+        g1[p] = ag_first(p)
+    y_oth3 = y_third(1 - czh, y_oth2)
+    for p in gb:
+        g2[p] = ag_second(p, g1[p])
+
+    arrive(y_own3)
+    arrive(g3[4])
+    gk = jnp.concatenate([cag[4, 16 * j:16 * j + 16, 512:640] for j in range(8)], axis=1)
+    gh, gl = split(gk)
+    ph, plow = split(yb[cy, czh].reshape(128, 1024))
+    ub[cc, cz, cy] = dot_split(jnp.concatenate([gh, gl], axis=0), ph, plow, NT)
+    u1 = [send(ub.at[cc, cz, cy], ub.at[cc, cz, cy], py[d]) for d in (1, 2, 3)]
+
+    def accumulate(p):
+        nb = 5 if p < 4 else 4
+        ch, cl = split(cag[p, :, :128 * nb] * scale)
+        out = dot_split(ystk[:, 128 * p:128 * p + 128], ch, cl)
+        for o in range(nb):
+            j = (p + o) % 8
+            f[:, 128 * j:128 * j + 128] += out[:, 128 * o:128 * o + 128]
+        f[:, 128 * p:128 * p + 128] += dot_split(
+            ystk[:, 128 * (p + 1):128 * (p + nb)], ch[:, 128:], cl[:, 128:], NT
+        )
+
+    f[...] = jnp.zeros_like(f)
+    accumulate(4)
+    for p in (5, 6, 7):
+        arrive(g3[p])
+        accumulate(p)
+    arrive(u1)
+    u2 = [send(ub.at[cc, cz], ub.at[cc, cz], pz[d]) for d in range(1, 8)]
+    for p in gb:
+        g3[p] = ag_third(p, g2[p])
+
+    arrive(y_oth3)
 
     def convert(i, carry):
         v = yb[i // 8, (i // 4) % 2, i % 4]
@@ -318,51 +408,14 @@
         v_a2a.append(send(vs.at[j], vr.at[my_j], peer))
     vr[my_j] = vs[my_j]
 
-    arrive(g2[4])
-    pr = pl.ds(pl.multiple_of((2 * cy + czh) * 128, 128), 128)
-    gk = jnp.concatenate([cag[4, 16 * j:16 * j + 16, 512:640] for j in range(8)], axis=1)
-    gh, gl = split(gk)
-    ub[cc, cz, cy] = dot_split(jnp.concatenate([gh, gl], axis=0), yh[pr], yl[pr], NT)
-    u1 = [send(ub.at[cc, cz, cy], ub.at[cc, cz, cy], py[d]) for d in (1, 2, 3)]
-
+    arrive(u2)
+    u3 = send(ub.at[cc], ub.at[cc], sibling)
+    for p in gb:
+        arrive(g3[p])
+        accumulate(p)
     arrive(v_a2a)
     for j in range(8):
-        f[:, 128 * j:128 * j + 128] = vr[j]
-
-    def accumulate(p):
-        nb = 5 if p < 4 else 4
-        ch, cl = split(cag[p, :, :128 * nb] * scale)
-        out = dot_split(ystk[:, 128 * p:128 * p + 128], ch, cl)
-        for o in range(nb):
-            j = (p + o) % 8
-            f[:, 128 * j:128 * j + 128] += out[:, 128 * o:128 * o + 128]
-        f[:, 128 * p:128 * p + 128] += dot_split(
-            ystk[:, 128 * (p + 1):128 * (p + nb)], ch[:, 128:], cl[:, 128:], NT
-        )
-
-    def u_step(s):
-        up, down = (cz - s) % 8, (cz + s) % 8
-        if s < 3:
-            u, w = ub.at[cc, up], ub.at[cc, down]
-        else:
-            u, w = ub.at[cc, up, pl.ds(0, 2)], ub.at[cc, down, pl.ds(2, 2)]
-        return [send(u, u, z_up), send(w, w, z_down)]
-
-    accumulate(4)
-    arrive(u1)
-    u2 = u_step(0)
-    for s, p in ((1, 5), (2, 6), (3, 7)):
-        arrive(g2[p])
-        accumulate(p)
-        arrive(u2)
-        u2 = u_step(s)
-    arrive(g2[0])
-    accumulate(0)
-    arrive(u2)
-    u3 = send(ub.at[cc], ub.at[cc], sibling)
-    for p in (1, 2, 3):
-        arrive(g2[p])
-        accumulate(p)
+        f[:, 128 * j:128 * j + 128] += vr[j]
 
     def times_root(m):
         mh, ml = split(m)
@@ -427,7 +480,9 @@
             pltpu.VMEM((1024, 1024), BF16),
             pltpu.VMEM((64, 1536), BF16),
             pltpu.VMEM((8, 128, 640), F32),
-            pltpu.VMEM((8, 3, 32, 640), F32),
+            pltpu.VMEM((8, 2, 16, 640), F32),
+            pltpu.VMEM((8, 2, 32, 640), F32),
+            pltpu.VMEM((8, 2, 32, 640), F32),
             pltpu.VMEM((8, 32, 640), F32),
             pltpu.VMEM((8, 3, 8, 640), F32),
             pltpu.VMEM((8, 32, 640), F32),

time: 124 us -> 102 us (0.82)
  Pallas kernels: 116 us -> 95.3 us
    pallas_call x1, Pallas kernels: 116 us -> 95.3 us  [body(): pl.pallas_call(functools.partial(kernel, tokens), out_shape=(jax.ShapeDty...]
where the time goes in v2:
time: 102 us; the launch traced here: 101 us
  Pallas kernels  95.3 us (93%)
  local copies, waits for them, and re-layouts  5 us (5%)
    pallas_call x1, Pallas kernels, body(): pl.pallas_call(functools.partial(kernel, tokens), out_shape=(jax.ShapeDty...  95.3 us
    unnamed x3, local copies, waits for them, and re-layouts  5 us

profile of v2, /device:TPU:1, one launch (start us, length us, event | category | flops | bytes accessed | tf_op | source)
XLA Modules:
  0.0 100.9 jit_solution(8456293986901276676)
XLA Ops:
  0.6 95.3 %kfac_step.1 = (f32[1,32,1024]{2,1,0:T(8,128)}, f32[1,32,1024]{2,1,0:T(8,128)}, f32[1,16,8192]{2,1,0:T(8,128)}) custom-call(s32[8]{0:T(128)} %order.1, s32[8]{0:T(128)} %refresh.1, bf16[1,4096,1024]{2,1,0:T(8,128)(2,1)} %x_hbm.1, bf16[16,4096]{1,0:T(8,128)(2,1)} %bitcast.3, f32[1,32,1024]{2,1,0:T(8,128)} %r_hbm.1, f32[1,32,1024]{2,1,0:T(8,128)} %y_hbm.1), custom_call_target="tpu_custom_call" | custom-call | flops 8000000000 | bytes 12000000 | tf_op jit(solution)/shard_map/kfac_step/pallas_call | solution.py:465
  95.9 1.6 %copy.12 = f32[1,32,1024]{2,1,0:T(8,128)} copy(f32[1,32,1024]{2,1,0:T(8,128)} %get-tuple-element.6) | data formatting | bytes 262144
  97.5 1.6 %copy.13 = f32[1,32,1024]{2,1,0:T(8,128)} copy(f32[1,32,1024]{2,1,0:T(8,128)} %get-tuple-element.7) | data formatting | bytes 262144
  99.0 1.9 %copy.14 = f32[1,16,8192]{2,1,0:T(8,128)} copy(f32[1,16,8192]{2,1,0:T(8,128)} %get-tuple-element.8) | data formatting | bytes 1048576

commit v3 on v2

--- a/solution.py
+++ b/solution.py
@@ -43,7 +43,7 @@
 def kernel(
     tokens,
     order, refresh, x_hbm, g_hbm, r_hbm, y_hbm,
-    fo, ro, uo,
+    both, uo,
     x, g, rsh, yb, yh, yl, ystk, pan, r0, t1, r1, s1, r2, zb0, zb1, sibs, sibr, cag,
     rcol, vs, vr, f, tb, ub, lsem, ssem, rsem,
 ):
@@ -307,6 +307,8 @@
     za = z_step(0, 0)
     for p in (2, 3):
         cm[p] = rs_mid(p, c1[p])
+    arrive(r_a2a)
+    r_y = [send(rcol.at[cy], rcol.at[cy], py[d]) for d in (1, 2, 3)]
     arrive(y_own1)
     y_own2 = y_second(czh)
     arrive(za)
@@ -335,8 +337,6 @@
     take(0)
     for p in ga:
         g1[p] = ag_first(p)
-    arrive(r_a2a)
-    r_y = [send(rcol.at[cy], rcol.at[cy], py[d]) for d in (1, 2, 3)]
     arrive(zc)
     zc = z_step(1, 3)
     for p in ga:
@@ -358,8 +358,9 @@
     gk = jnp.concatenate([cag[4, 16 * j:16 * j + 16, 512:640] for j in range(8)], axis=1)
     gh, gl = split(gk)
     ph, plow = split(yb[cy, czh].reshape(128, 1024))
-    ub[cc, cz, cy] = dot_split(jnp.concatenate([gh, gl], axis=0), ph, plow, NT)
-    u1 = [send(ub.at[cc, cz, cy], ub.at[cc, cz, cy], py[d]) for d in (1, 2, 3)]
+    cond = dot_split(jnp.concatenate([gh, gl], axis=0), ph, plow, NT)
+    ub[cc, cz, cy] = cond
+    u1 = [send(ub.at[cc, cz, cy], ub.at[cc, cz, cy], pz[d]) for d in range(1, 8)]
 
     def accumulate(p):
         nb = 5 if p < 4 else 4
@@ -378,7 +379,7 @@
         arrive(g3[p])
         accumulate(p)
     arrive(u1)
-    u2 = [send(ub.at[cc, cz], ub.at[cc, cz], pz[d]) for d in range(1, 8)]
+    u2 = [send(ub.at[cc, :, cy], ub.at[cc, :, cy], py[d]) for d in (1, 2, 3)]
     for p in gb:
         g3[p] = ag_third(p, g2[p])
 
@@ -423,7 +424,7 @@
 
     third = times_root(times_root(f[...]))
     yr = yb[cy, czh, cx]
-    ro[0] = jnp.where(refresh[b_mine] == 1, 1.5 * yr - 0.5 * third, yr)
+    both[1] = jnp.where(refresh[b_mine] == 1, 1.5 * yr - 0.5 * third, yr)
 
     panel = 2 * cy + czh
     rows_x = pl.ds(pl.multiple_of(cx * 32, 32), 32)
@@ -442,7 +443,7 @@
         else:
             c = turned(cag[j, :, 128 * (8 - o):128 * (8 - o) + 128])
         at = pl.ds(pl.multiple_of(j * 128, 128), 128)
-        fo[0, :, at] = DECAY * rsh[:, at] + scale * c
+        both[0, :, at] = DECAY * rsh[:, at] + scale * c
 
     u3.wait_recv()
     for b in range(8):
@@ -462,15 +463,14 @@
     hbm = pl.BlockSpec(memory_space=pl.ANY)
     smem = pl.BlockSpec(memory_space=pltpu.SMEM)
     vmem = pl.BlockSpec(memory_space=pltpu.VMEM)
-    return pl.pallas_call(
+    both, update = pl.pallas_call(
         functools.partial(kernel, tokens),
         out_shape=(
-            jax.ShapeDtypeStruct((1, 32, 1024), F32),
-            jax.ShapeDtypeStruct((1, 32, 1024), F32),
+            jax.ShapeDtypeStruct((2, 32, 1024), F32),
             jax.ShapeDtypeStruct((1, 16, D), F32),
         ),
         in_specs=[smem, smem, hbm, hbm, hbm, hbm],
-        out_specs=(vmem, vmem, vmem),
+        out_specs=(vmem, vmem),
         scratch_shapes=[
             pltpu.VMEM((tokens_here, 1024), BF16),
             pltpu.VMEM((16, tokens_here), BF16),
@@ -513,6 +513,7 @@
         running_factor_blocks,
         inverse_root_blocks,
     )
+    return both[0:1], both[1:2], update
 
 
 def solution(mesh):

time: 102 us -> 100 us (0.980)
  local copies, waits for them, and re-layouts: 5 us -> 3.55 us
    unnamed x3 -> x1, local copies, waits for them, and re-layouts: 5 us -> 1.87 us
    slice x0 -> x1, local copies, waits for them, and re-layouts: none -> 1.69 us  [body(): return (both[0:1], both[1:2], update)]
where the time goes in v3:
time: 100 us; the launch traced here: 99.2 us
  Pallas kernels  95 us (95%)
  local copies, waits for them, and re-layouts  3.55 us (4%)
    pallas_call x1, Pallas kernels, body(): pl.pallas_call(functools.partial(kernel, tokens), out_shape=(jax.ShapeDty...  95 us

profile of v3, /device:TPU:1, one launch (start us, length us, event | category | flops | bytes accessed | tf_op | source)
XLA Modules:
  0.0 99.2 jit_solution(13513864797564194113)
XLA Ops:
  0.6 95.0 %kfac_step.1 = (f32[2,32,1024]{2,1,0:T(8,128)}, f32[1,16,8192]{2,1,0:T(8,128)}) custom-call(s32[8]{0:T(128)} %order.1, s32[8]{0:T(128)} %refresh.1, bf16[1,4096,1024]{2,1,0:T(8,128)(2,1)} %x_hbm.1, bf16[16,4096]{1,0:T(8,128)(2,1)} %bitcast.3, f32[1,32,1024]{2,1,0:T(8,128)} %r_hbm.1, f32[1,32,1024]{2,1,0:T(8,128)} %y_hbm.1), custom_call_target="tpu_custom_call" | custom-call | flops 8000000000 | bytes 12000000 | tf_op jit(solution)/shard_map/kfac_step/pallas_call | solution.py:466
  95.6 1.7 %fusion = (f32[1,32,1024]{2,1,0:T(8,128)}, f32[1,32,1024]{2,1,0:T(8,128)}) fusion(f32[2,32,1024]{2,1,0:T(8,128)} %get-tuple-element.5), kind=kLoop, calls=%fused_computation | loop fusion | bytes 524288 | tf_op jit(solution)/shard_map/slice | solution.py:516
  97.3 1.9 %copy.10 = f32[1,16,8192]{2,1,0:T(8,128)} copy(f32[1,16,8192]{2,1,0:T(8,128)} %get-tuple-element.14) | data formatting | bytes 1048576

commit v4 on v3

--- a/solution.py
+++ b/solution.py
@@ -281,13 +281,13 @@
         pan[4, 16 * j:16 * j + 16, 512:640] = grads[:, 128 * j:128 * j + 128]
     for p in (4, 5):
         c1[p] = rs_first(p)
-    y_z.wait_recv()
-    y_oth1 = y_first(1 - czh)
     gemm(3, 0, x.shape[0], True)
     for p in (6, 7):
         c1[p] = rs_first(p)
     for p in (4, 5):
         cm[p] = rs_mid(p, c1[p])
+    y_z.wait_recv()
+    y_oth1 = y_first(1 - czh)
     gemm(0, 0, x.shape[0], True)
     for p in (0, 1):
         c1[p] = rs_first(p)

time: 100 us -> 96.4 us (0.964)
  Pallas kernels: 95 us -> 91.3 us
    pallas_call x1, Pallas kernels: 95 us -> 91.3 us  [body(): pl.pallas_call(functools.partial(kernel, tokens), out_shape=(jax.ShapeDty...]
where the time goes in v4:
time: 96.4 us; the launch traced here: 95.5 us
  Pallas kernels  91.3 us (95%)
  local copies, waits for them, and re-layouts  3.55 us (4%)
    pallas_call x1, Pallas kernels, body(): pl.pallas_call(functools.partial(kernel, tokens), out_shape=(jax.ShapeDty...  91.3 us

profile of v4, /device:TPU:1, one launch (start us, length us, event | category | flops | bytes accessed | tf_op | source)
XLA Modules:
  0.0 95.5 jit_solution(17838366583869997415)
XLA Ops:
  0.6 91.3 %kfac_step.1 = (f32[2,32,1024]{2,1,0:T(8,128)}, f32[1,16,8192]{2,1,0:T(8,128)}) custom-call(s32[8]{0:T(128)} %order.1, s32[8]{0:T(128)} %refresh.1, bf16[1,4096,1024]{2,1,0:T(8,128)(2,1)} %x_hbm.1, bf16[16,4096]{1,0:T(8,128)(2,1)} %bitcast.3, f32[1,32,1024]{2,1,0:T(8,128)} %r_hbm.1, f32[1,32,1024]{2,1,0:T(8,128)} %y_hbm.1), custom_call_target="tpu_custom_call" | custom-call | flops 8000000000 | bytes 12000000 | tf_op jit(solution)/shard_map/kfac_step/pallas_call | solution.py:466
  92.0 1.7 %fusion = (f32[1,32,1024]{2,1,0:T(8,128)}, f32[1,32,1024]{2,1,0:T(8,128)}) fusion(f32[2,32,1024]{2,1,0:T(8,128)} %get-tuple-element.5), kind=kLoop, calls=%fused_computation | loop fusion | bytes 524288 | tf_op jit(solution)/shard_map/slice | solution.py:516
  93.7 1.9 %copy.10 = f32[1,16,8192]{2,1,0:T(8,128)} copy(f32[1,16,8192]{2,1,0:T(8,128)} %get-tuple-element.14) | data formatting | bytes 1048576
